TPU v7x, 128 devices: a whole 4x4x4 slice. The times are simulated.
128 devices in a mesh: row: 8 (over z, x_lo), col: 16 (over x_hi, y, core).
Axes of the slice: x: 4 (x_hi: 2, x_lo: 2; x = x_hi * 2 + x_lo), y: 4, z: 4, core: 2. Of those that a mesh axis runs over, the one named last changes fastest.
Arguments:
- eigen_basis_rows: float32 [16384, 8192], P('row', 'col'), may hold values from -6 to 6
- mirror_entries: float32 [6, 8, 128, 2176], P(None, 'row', 'col'), may hold values from -0.125 to 0.125
- tau_coefficients: float32 [6, 8, 128], P(None, 'row', 'col'), may hold values from 0.5 to 2
- mirror_tallies: int32 [6, 8], P(None, 'row'), may hold values from 32 to 128
Outputs:
- transformed: float32 [16384, 8192], P('row', 'col')
All inputs are finite; a program needn't handle non-finite values.
Results may differ from a plain program's by a relative error of at most 0.00017.
Values sent between devices are 32-bit elements; how exact they have to be, the bound alone decides.
A program may use at most 64 MiB of HBM per device.

v0:
```python
import jax
import jax.numpy as jnp
from jax import lax
from jax.sharding import PartitionSpec as P

PRECISE = lax.Precision.HIGHEST


def shifted(block, axis, distance):
    devices = range(lax.axis_size(axis))
    route = [(i - distance, i) for i in devices if i - distance in devices]
    return lax.ppermute(block, axis, route)


def storage_triangle(mirror_directions, scaling, retention_flags):
    gram_matrix = lax.dot_general(
        mirror_directions,
        mirror_directions,
        (((1,), (1,)), ((), ())),
        precision=PRECISE,
        preferred_element_type=jnp.float32,
    )
    diag_inverse = jnp.where(retention_flags, scaling, jnp.ones_like(scaling))
    nilpotent = diag_inverse[:, None] * jnp.triu(gram_matrix, 1)
    order_count = mirror_directions.shape[0]
    identity = jnp.eye(order_count, dtype=jnp.float32)
    power_term = -nilpotent
    inverse_part = identity + power_term
    reached = 1
    while 2 * reached < order_count:
        power_term = jnp.dot(
            power_term, power_term, precision=PRECISE, preferred_element_type=jnp.float32
        )
        inverse_part = inverse_part + jnp.dot(
            inverse_part, power_term, precision=PRECISE, preferred_element_type=jnp.float32
        )
        reached = reached * 2
    return inverse_part * diag_inverse[None, :]


def apply_block(window, mirror_directions, triangle_operator):
    coeffs = jnp.dot(
        mirror_directions, window, precision=PRECISE, preferred_element_type=jnp.float32
    )
    mixed_terms = jnp.dot(
        triangle_operator, coeffs, precision=PRECISE, preferred_element_type=jnp.float32
    )
    return window - lax.dot_general(
        mirror_directions,
        mixed_terms,
        (((0,), (0,)), ((), ())),
        precision=PRECISE,
        preferred_element_type=jnp.float32,
    )


def per_device(eigen_basis_rows, mirror_entries, tau_coefficients, mirror_tallies):
    gathered, scale_all = (
        lax.all_gather(mirror_entries, "col", axis=2, tiled=True),
        lax.all_gather(tau_coefficients, "col", axis=2, tiled=True),
    )
    householders = gathered[:, 0]
    scale_rows = scale_all[:, 0]
    live_counts = mirror_tallies[:, 0]
    row_count = eigen_basis_rows.shape[0]
    group_count, width_rows, window_rows = householders.shape
    sections = lax.axis_size("row")
    position = lax.axis_index("row")
    slot_index = lax.iota(jnp.int32, width_rows)
    cell_index = lax.iota(jnp.int32, window_rows)
    retention_flags = slot_index[None, :] < live_counts[:, None]
    row_keep = (cell_index < row_count) | (position != sections - 1)
    householders = (
        householders
        * retention_flags[:, :, None].astype(jnp.float32)
        * row_keep[None, None, :].astype(jnp.float32)
    )
    factors = jax.vmap(storage_triangle)(householders, scale_rows, retention_flags)
    total_steps = 2 * (group_count - 1) + sections

    def plan(step_index, panel_ordinal):
        offset = step_index - panel_ordinal
        active = (offset >= 0) & (offset % 2 == 0) & (offset // 2 < group_count)
        return (active, jnp.clip(offset // 2, 0, group_count - 1))

    def advance(step_index, current):
        below_rows = shifted(current[:width_rows], "row", -1)
        active, batch_ordinal = plan(step_index, position)

        def working(state):
            window = jnp.concatenate([state, below_rows], axis=0)
            mirror_directions = lax.dynamic_index_in_dim(
                householders, batch_ordinal, 0, keepdims=False
            )
            triangle_operator = lax.dynamic_index_in_dim(factors, batch_ordinal, 0, keepdims=False)
            updated = apply_block(window, mirror_directions, triangle_operator)
            return (updated[:row_count], updated[row_count:])

        def waiting(state):
            return (state, below_rows)

        current, returned = lax.cond(active, working, waiting, current)
        arrived = shifted(returned, "row", 1)
        sender_active, unused = plan(step_index, position - 1)
        sender_active = sender_active & (position > 0)
        top_rows = jnp.where(sender_active, arrived, current[:width_rows])
        return lax.dynamic_update_slice_in_dim(current, top_rows, 0, 0)

    return lax.fori_loop(0, total_steps, advance, eigen_basis_rows)


def solution(mesh):
    in_specs = (P("row", "col"), P(None, "row", "col", None), P(None, "row", "col"), P(None, "row"))
    out_specs = P("row", "col")
    return jax.shard_map(
        per_device, mesh=mesh, in_specs=in_specs, out_specs=out_specs, check_vma=False
    )
```

profile of v0, /device:TPU:98, one launch (start us, length us, event | category | flops | bytes accessed | tf_op | source)
XLA Modules:
  0.0 718.3 jit_solution(6473481367738353305)
XLA Ops:
  6.5 4.7 copy.26
  11.4 23.7 %all_gather.7 = f32[6,1,128]{0,1,2:T(1,128)S(1)} all-gather(f32[6,1,8]{0,1,2:T(1,128)S(1)} %copy.8), channel_id=1, replica_groups=mesh['row'=8,'col'=16] {'col'}, dimensions={2}, use_global_device_ids=true | all-gather | bytes 3264 | tf_op jit(solution)/shard_map/all_gather | solution.py:60
  35.4 42.0 %all-gather.2.cloned.1.call-done = f32[6,1,128,2176]{3,2,0,1:T(8,128)} async-done(((f32[6,1,8,2176]{3,2,0,1:T(8,128)}), f32[6,1,128,2176]{3,2,0,1:T(8,128)}) %all-gather.2.cloned.1.call-update) | async-done | bytes 6684688 | tf_op jit(solution)/shard_map/all_gather | solution.py:59
  80.9 6.6 fusion.13
  94.1 617.3 %while.16 = (s32[]{:T(128)}, f32[2048,512]{1,0:T(8,128)}, s32[]{:T(128)}, f32[6,128,2176]{2,1,0:T(8,128)}, f32[6,128,128]{2,1,0:T(8,128)S(1)}, /*index=5*/s32[]{...) while((s32[]{:T(128)}, f32[2048,512]{1,0:T(8,128)}, s32[]{:T(128)}, ...), condition=%wide.region_3.4_spmd, body=%wide.region_0.3_spmd.sunk | while | flops 3524395008 | bytes 38470408 | solution.py:109
  98.5 5.9 collective-permute-done
  106.8 9.0 %collective-permute-done.1 = f32[128,512]{1,0:T(8,128)S(1)} collective-permute-done((f32[128,512]{1,0:T(8,128)S(1)}, f32[128,512]{1,0:T(8,128)S(1)}, u32[]{:S(2)}, u32[]{:S(2)}) %collective-permute-start.1) | collective-permute-done | bytes 262176 | tf_op jit(solution)/shard_map/while/body/eval_jaxpr/ppermute | solution.py:12
  117.4 4.6 collective-permute-start
  122.0 4.2 collective-permute-done
  128.6 7.4 %collective-permute-done.1 = f32[128,512]{1,0:T(8,128)S(1)} collective-permute-done((f32[128,512]{1,0:T(8,128)S(1)}, f32[128,512]{1,0:T(8,128)S(1)}, u32[]{:S(2)}, u32[]{:S(2)}) %collective-permute-start.1) | collective-permute-done | bytes 262176 | tf_op jit(solution)/shard_map/while/body/eval_jaxpr/ppermute | solution.py:12
  137.7 4.8 collective-permute-start
  148.7 7.4 %collective-permute-done.1 = f32[128,512]{1,0:T(8,128)S(1)} collective-permute-done((f32[128,512]{1,0:T(8,128)S(1)}, f32[128,512]{1,0:T(8,128)S(1)}, u32[]{:S(2)}, u32[]{:S(2)}) %collective-permute-start.1) | collective-permute-done | bytes 262176 | tf_op jit(solution)/shard_map/while/body/eval_jaxpr/ppermute | solution.py:12
  157.8 4.8 collective-permute-start
  168.8 13.5 %collective-permute-done.1 = f32[128,512]{1,0:T(8,128)S(1)} collective-permute-done((f32[128,512]{1,0:T(8,128)S(1)}, f32[128,512]{1,0:T(8,128)S(1)}, u32[]{:S(2)}, u32[]{:S(2)}) %collective-permute-start.1) | collective-permute-done | bytes 262176 | tf_op jit(solution)/shard_map/while/body/eval_jaxpr/ppermute | solution.py:12
  184.0 18.7 %collective-permute-start = (f32[128,512]{1,0:T(8,128)S(1)}, f32[128,512]{1,0:T(8,128)S(1)}, u32[]{:S(2)}, u32[]{:S(2)}) collective-permute-start(f32[128,512]{1,0:T(8,128)S(1)} %slice.40), channel_id=1, source_target_pairs={{16,0},{32,16},{48,32},{64,48},{80,64},{96,80},{112,96},{17,1},{33... | collective-permute-start | bytes 786440 | tf_op jit(solution)/shard_map/while/body/eval_jaxpr/ppermute | solution.py:12
  208.9 21.9 %collective-permute-done.1 = f32[128,512]{1,0:T(8,128)S(1)} collective-permute-done((f32[128,512]{1,0:T(8,128)S(1)}, f32[128,512]{1,0:T(8,128)S(1)}, u32[]{:S(2)}, u32[]{:S(2)}) %collective-permute-start.1) | collective-permute-done | bytes 262176 | tf_op jit(solution)/shard_map/while/body/eval_jaxpr/ppermute | solution.py:12
  232.5 20.5 %collective-permute-start = (f32[128,512]{1,0:T(8,128)S(1)}, f32[128,512]{1,0:T(8,128)S(1)}, u32[]{:S(2)}, u32[]{:S(2)}) collective-permute-start(f32[128,512]{1,0:T(8,128)S(1)} %slice.40), channel_id=1, source_target_pairs={{16,0},{32,16},{48,32},{64,48},{80,64},{96,80},{112,96},{17,1},{33... | collective-permute-start | bytes 786440 | tf_op jit(solution)/shard_map/while/body/eval_jaxpr/ppermute | solution.py:12
  259.3 21.7 %collective-permute-done.1 = f32[128,512]{1,0:T(8,128)S(1)} collective-permute-done((f32[128,512]{1,0:T(8,128)S(1)}, f32[128,512]{1,0:T(8,128)S(1)}, u32[]{:S(2)}, u32[]{:S(2)}) %collective-permute-start.1) | collective-permute-done | bytes 262176 | tf_op jit(solution)/shard_map/while/body/eval_jaxpr/ppermute | solution.py:12
  282.7 18.7 %collective-permute-start = (f32[128,512]{1,0:T(8,128)S(1)}, f32[128,512]{1,0:T(8,128)S(1)}, u32[]{:S(2)}, u32[]{:S(2)}) collective-permute-start(f32[128,512]{1,0:T(8,128)S(1)} %slice.40), channel_id=1, source_target_pairs={{16,0},{32,16},{48,32},{64,48},{80,64},{96,80},{112,96},{17,1},{33... | collective-permute-start | bytes 786440 | tf_op jit(solution)/shard_map/while/body/eval_jaxpr/ppermute | solution.py:12
  307.6 21.6 %collective-permute-done.1 = f32[128,512]{1,0:T(8,128)S(1)} collective-permute-done((f32[128,512]{1,0:T(8,128)S(1)}, f32[128,512]{1,0:T(8,128)S(1)}, u32[]{:S(2)}, u32[]{:S(2)}) %collective-permute-start.1) | collective-permute-done | bytes 262176 | tf_op jit(solution)/shard_map/while/body/eval_jaxpr/ppermute | solution.py:12
  331.0 4.8 collective-permute-start
  339.7 14.4 %conditional.2 = (f32[2048,512]{1,0:T(8,128)}, f32[128,512]{1,0:T(8,128)S(1)}, f32[128,512]{1,0:T(8,128)S(1)}) conditional(s32[]{:T(128)} %convert_element_type.41, (f32[2048,512]{1,0:T(8,128)}, f32[128,512]{1,0:T(8,128)S(1)}) %tuple.59, (f32[2048,512]{1,0:T(8,128)}, f32[128,512]{1,0:T(8,128)S(1)}, s32[]{:T(128)}, f32[6,128,2176]{2,1,0:T(8,128)}, ...), branch_computations={%region_1.1_spmd, %region_2.2_spmd} | conditional | flops 3524329472 | bytes 35061820 | solution.py:102
  342.3 3.9 fusion.1
  346.6 5.0 convolution_subtract_fusion
  355.4 6.9 collective-permute-done.1
  364.0 6.0 collective-permute-start
  376.2 20.8 %collective-permute-done.1 = f32[128,512]{1,0:T(8,128)S(1)} collective-permute-done((f32[128,512]{1,0:T(8,128)S(1)}, f32[128,512]{1,0:T(8,128)S(1)}, u32[]{:S(2)}, u32[]{:S(2)}) %collective-permute-start.1) | collective-permute-done | bytes 262176 | tf_op jit(solution)/shard_map/while/body/eval_jaxpr/ppermute | solution.py:12
  398.7 4.8 collective-permute-start
  407.4 14.4 %conditional.2 = (f32[2048,512]{1,0:T(8,128)}, f32[128,512]{1,0:T(8,128)S(1)}, f32[128,512]{1,0:T(8,128)S(1)}) conditional(s32[]{:T(128)} %convert_element_type.41, (f32[2048,512]{1,0:T(8,128)}, f32[128,512]{1,0:T(8,128)S(1)}) %tuple.59, (f32[2048,512]{1,0:T(8,128)}, f32[128,512]{1,0:T(8,128)S(1)}, s32[]{:T(128)}, f32[6,128,2176]{2,1,0:T(8,128)}, ...), branch_computations={%region_1.1_spmd, %region_2.2_spmd} | conditional | flops 3524329472 | bytes 35061820 | solution.py:102
  410.1 3.9 fusion.1
  414.3 5.0 convolution_subtract_fusion
  423.2 6.9 collective-permute-done.1
  431.8 5.5 collective-permute-start
  443.5 20.8 %collective-permute-done.1 = f32[128,512]{1,0:T(8,128)S(1)} collective-permute-done((f32[128,512]{1,0:T(8,128)S(1)}, f32[128,512]{1,0:T(8,128)S(1)}, u32[]{:S(2)}, u32[]{:S(2)}) %collective-permute-start.1) | collective-permute-done | bytes 262176 | tf_op jit(solution)/shard_map/while/body/eval_jaxpr/ppermute | solution.py:12
  466.1 4.8 collective-permute-start
  470.9 4.3 collective-permute-done
  475.3 14.4 %conditional.2 = (f32[2048,512]{1,0:T(8,128)}, f32[128,512]{1,0:T(8,128)S(1)}, f32[128,512]{1,0:T(8,128)S(1)}) conditional(s32[]{:T(128)} %convert_element_type.41, (f32[2048,512]{1,0:T(8,128)}, f32[128,512]{1,0:T(8,128)S(1)}) %tuple.59, (f32[2048,512]{1,0:T(8,128)}, f32[128,512]{1,0:T(8,128)S(1)}, s32[]{:T(128)}, f32[6,128,2176]{2,1,0:T(8,128)}, ...), branch_computations={%region_1.1_spmd, %region_2.2_spmd} | conditional | flops 3524329472 | bytes 35061820 | solution.py:102
  477.9 3.9 fusion.1
  482.2 5.0 convolution_subtract_fusion
  491.0 7.8 %collective-permute-done.1 = f32[128,512]{1,0:T(8,128)S(1)} collective-permute-done((f32[128,512]{1,0:T(8,128)S(1)}, f32[128,512]{1,0:T(8,128)S(1)}, u32[]{:S(2)}, u32[]{:S(2)}) %collective-permute-start.1) | collective-permute-done | bytes 262176 | tf_op jit(solution)/shard_map/while/body/eval_jaxpr/ppermute | solution.py:12
  500.5 4.2 collective-permute-start
  504.8 5.7 collective-permute-done
  512.8 23.2 %collective-permute-done.1 = f32[128,512]{1,0:T(8,128)S(1)} collective-permute-done((f32[128,512]{1,0:T(8,128)S(1)}, f32[128,512]{1,0:T(8,128)S(1)}, u32[]{:S(2)}, u32[]{:S(2)}) %collective-permute-start.1) | collective-permute-done | bytes 262176 | tf_op jit(solution)/shard_map/while/body/eval_jaxpr/ppermute | solution.py:12
  537.8 6.4 collective-permute-start
  544.2 5.6 collective-permute-done
  549.8 14.4 %conditional.2 = (f32[2048,512]{1,0:T(8,128)}, f32[128,512]{1,0:T(8,128)S(1)}, f32[128,512]{1,0:T(8,128)S(1)}) conditional(s32[]{:T(128)} %convert_element_type.41, (f32[2048,512]{1,0:T(8,128)}, f32[128,512]{1,0:T(8,128)S(1)}) %tuple.59, (f32[2048,512]{1,0:T(8,128)}, f32[128,512]{1,0:T(8,128)S(1)}, s32[]{:T(128)}, f32[6,128,2176]{2,1,0:T(8,128)}, ...), branch_computations={%region_1.1_spmd, %region_2.2_spmd} | conditional | flops 3524329472 | bytes 35061820 | solution.py:102
  552.5 3.9 fusion.1
  556.7 5.0 convolution_subtract_fusion
  565.6 8.5 %collective-permute-done.1 = f32[128,512]{1,0:T(8,128)S(1)} collective-permute-done((f32[128,512]{1,0:T(8,128)S(1)}, f32[128,512]{1,0:T(8,128)S(1)}, u32[]{:S(2)}, u32[]{:S(2)}) %collective-permute-start.1) | collective-permute-done | bytes 262176 | tf_op jit(solution)/shard_map/while/body/eval_jaxpr/ppermute | solution.py:12
  575.8 4.6 collective-permute-start
  580.4 5.6 collective-permute-done
  588.3 21.2 %collective-permute-done.1 = f32[128,512]{1,0:T(8,128)S(1)} collective-permute-done((f32[128,512]{1,0:T(8,128)S(1)}, f32[128,512]{1,0:T(8,128)S(1)}, u32[]{:S(2)}, u32[]{:S(2)}) %collective-permute-start.1) | collective-permute-done | bytes 262176 | tf_op jit(solution)/shard_map/while/body/eval_jaxpr/ppermute | solution.py:12
  611.2 4.4 collective-permute-start
  619.5 14.4 %conditional.2 = (f32[2048,512]{1,0:T(8,128)}, f32[128,512]{1,0:T(8,128)S(1)}, f32[128,512]{1,0:T(8,128)S(1)}) conditional(s32[]{:T(128)} %convert_element_type.41, (f32[2048,512]{1,0:T(8,128)}, f32[128,512]{1,0:T(8,128)S(1)}) %tuple.59, (f32[2048,512]{1,0:T(8,128)}, f32[128,512]{1,0:T(8,128)S(1)}, s32[]{:T(128)}, f32[6,128,2176]{2,1,0:T(8,128)}, ...), branch_computations={%region_1.1_spmd, %region_2.2_spmd} | conditional | flops 3524329472 | bytes 35061820 | solution.py:102
  622.2 3.9 fusion.1
  626.4 5.0 convolution_subtract_fusion
  635.3 9.1 %collective-permute-done.1 = f32[128,512]{1,0:T(8,128)S(1)} collective-permute-done((f32[128,512]{1,0:T(8,128)S(1)}, f32[128,512]{1,0:T(8,128)S(1)}, u32[]{:S(2)}, u32[]{:S(2)}) %collective-permute-start.1) | collective-permute-done | bytes 262176 | tf_op jit(solution)/shard_map/while/body/eval_jaxpr/ppermute | solution.py:12
  646.1 4.6 collective-permute-start
  656.8 20.8 %collective-permute-done.1 = f32[128,512]{1,0:T(8,128)S(1)} collective-permute-done((f32[128,512]{1,0:T(8,128)S(1)}, f32[128,512]{1,0:T(8,128)S(1)}, u32[]{:S(2)}, u32[]{:S(2)}) %collective-permute-start.1) | collective-permute-done | bytes 262176 | tf_op jit(solution)/shard_map/while/body/eval_jaxpr/ppermute | solution.py:12
  679.3 4.8 collective-permute-start
  688.0 14.4 %conditional.2 = (f32[2048,512]{1,0:T(8,128)}, f32[128,512]{1,0:T(8,128)S(1)}, f32[128,512]{1,0:T(8,128)S(1)}) conditional(s32[]{:T(128)} %convert_element_type.41, (f32[2048,512]{1,0:T(8,128)}, f32[128,512]{1,0:T(8,128)S(1)}) %tuple.59, (f32[2048,512]{1,0:T(8,128)}, f32[128,512]{1,0:T(8,128)S(1)}, s32[]{:T(128)}, f32[6,128,2176]{2,1,0:T(8,128)}, ...), branch_computations={%region_1.1_spmd, %region_2.2_spmd} | conditional | flops 3524329472 | bytes 35061820 | solution.py:102
  690.7 3.9 fusion.1
  694.9 5.0 convolution_subtract_fusion
  703.8 6.9 collective-permute-done.1
  (152 shorter events, 169.8 us)
Async XLA Ops:
  6.5 4.7 copy-start.1
  6.5 4.8 copy-start.2
  6.5 70.9 %all-gather.2.cloned.1.call-start = ((), (), s32[]{:S(2)}) async-start(), calls=%async_computation | async-start | bytes 7102464 | tf_op jit(solution)/shard_map/all_gather | solution.py:59
  80.9 6.6 copy-start
  95.1 9.3 %collective-permute-start = (f32[128,512]{1,0:T(8,128)S(1)}, f32[128,512]{1,0:T(8,128)S(1)}, u32[]{:S(2)}, u32[]{:S(2)}) collective-permute-start(f32[128,512]{1,0:T(8,128)S(1)} %slice.40), channel_id=1, source_target_pairs={{16,0},{32,16},{48,32},{64,48},{80,64},{96,80},{112,96},{17,1},{33... | collective-permute-start | bytes 786440 | tf_op jit(solution)/shard_map/while/body/eval_jaxpr/ppermute | solution.py:12
  105.4 10.3 %collective-permute-start.1 = (f32[128,512]{1,0:T(8,128)S(1)}, f32[128,512]{1,0:T(8,128)S(1)}, u32[]{:S(2)}, u32[]{:S(2)}) collective-permute-start(f32[128,512]{1,0:T(8,128)S(1)} %get-tuple-element.288), channel_id=1, source_target_pairs={{0,16},{16,32},{32,48},{48,64},{64,80},{80,96},{96,112},{1,17},{17... | collective-permute-start | bytes 786440 | tf_op jit(solution)/shard_map/while/body/eval_jaxpr/ppermute | solution.py:12
  117.4 8.8 %collective-permute-start = (f32[128,512]{1,0:T(8,128)S(1)}, f32[128,512]{1,0:T(8,128)S(1)}, u32[]{:S(2)}, u32[]{:S(2)}) collective-permute-start(f32[128,512]{1,0:T(8,128)S(1)} %slice.40), channel_id=1, source_target_pairs={{16,0},{32,16},{48,32},{64,48},{80,64},{96,80},{112,96},{17,1},{33... | collective-permute-start | bytes 786440 | tf_op jit(solution)/shard_map/while/body/eval_jaxpr/ppermute | solution.py:12
  127.2 8.7 %collective-permute-start.1 = (f32[128,512]{1,0:T(8,128)S(1)}, f32[128,512]{1,0:T(8,128)S(1)}, u32[]{:S(2)}, u32[]{:S(2)}) collective-permute-start(f32[128,512]{1,0:T(8,128)S(1)} %get-tuple-element.288), channel_id=1, source_target_pairs={{0,16},{16,32},{32,48},{48,64},{64,80},{80,96},{96,112},{1,17},{17... | collective-permute-start | bytes 786440 | tf_op jit(solution)/shard_map/while/body/eval_jaxpr/ppermute | solution.py:12
  137.7 8.7 %collective-permute-start = (f32[128,512]{1,0:T(8,128)S(1)}, f32[128,512]{1,0:T(8,128)S(1)}, u32[]{:S(2)}, u32[]{:S(2)}) collective-permute-start(f32[128,512]{1,0:T(8,128)S(1)} %slice.40), channel_id=1, source_target_pairs={{16,0},{32,16},{48,32},{64,48},{80,64},{96,80},{112,96},{17,1},{33... | collective-permute-start | bytes 786440 | tf_op jit(solution)/shard_map/while/body/eval_jaxpr/ppermute | solution.py:12
  147.3 8.7 %collective-permute-start.1 = (f32[128,512]{1,0:T(8,128)S(1)}, f32[128,512]{1,0:T(8,128)S(1)}, u32[]{:S(2)}, u32[]{:S(2)}) collective-permute-start(f32[128,512]{1,0:T(8,128)S(1)} %get-tuple-element.288), channel_id=1, source_target_pairs={{0,16},{16,32},{32,48},{48,64},{64,80},{80,96},{96,112},{1,17},{17... | collective-permute-start | bytes 786440 | tf_op jit(solution)/shard_map/while/body/eval_jaxpr/ppermute | solution.py:12
  157.8 8.7 %collective-permute-start = (f32[128,512]{1,0:T(8,128)S(1)}, f32[128,512]{1,0:T(8,128)S(1)}, u32[]{:S(2)}, u32[]{:S(2)}) collective-permute-start(f32[128,512]{1,0:T(8,128)S(1)} %slice.40), channel_id=1, source_target_pairs={{16,0},{32,16},{48,32},{64,48},{80,64},{96,80},{112,96},{17,1},{33... | collective-permute-start | bytes 786440 | tf_op jit(solution)/shard_map/while/body/eval_jaxpr/ppermute | solution.py:12
  167.5 14.8 %collective-permute-start.1 = (f32[128,512]{1,0:T(8,128)S(1)}, f32[128,512]{1,0:T(8,128)S(1)}, u32[]{:S(2)}, u32[]{:S(2)}) collective-permute-start(f32[128,512]{1,0:T(8,128)S(1)} %get-tuple-element.288), channel_id=1, source_target_pairs={{0,16},{16,32},{32,48},{48,64},{64,80},{80,96},{96,112},{1,17},{17... | collective-permute-start | bytes 786440 | tf_op jit(solution)/shard_map/while/body/eval_jaxpr/ppermute | solution.py:12
  184.0 22.6 %collective-permute-start = (f32[128,512]{1,0:T(8,128)S(1)}, f32[128,512]{1,0:T(8,128)S(1)}, u32[]{:S(2)}, u32[]{:S(2)}) collective-permute-start(f32[128,512]{1,0:T(8,128)S(1)} %slice.40), channel_id=1, source_target_pairs={{16,0},{32,16},{48,32},{64,48},{80,64},{96,80},{112,96},{17,1},{33... | collective-permute-start | bytes 786440 | tf_op jit(solution)/shard_map/while/body/eval_jaxpr/ppermute | solution.py:12
  207.6 23.3 %collective-permute-start.1 = (f32[128,512]{1,0:T(8,128)S(1)}, f32[128,512]{1,0:T(8,128)S(1)}, u32[]{:S(2)}, u32[]{:S(2)}) collective-permute-start(f32[128,512]{1,0:T(8,128)S(1)} %get-tuple-element.288), channel_id=1, source_target_pairs={{0,16},{16,32},{32,48},{48,64},{64,80},{80,96},{96,112},{1,17},{17... | collective-permute-start | bytes 786440 | tf_op jit(solution)/shard_map/while/body/eval_jaxpr/ppermute | solution.py:12
  232.5 24.4 %collective-permute-start = (f32[128,512]{1,0:T(8,128)S(1)}, f32[128,512]{1,0:T(8,128)S(1)}, u32[]{:S(2)}, u32[]{:S(2)}) collective-permute-start(f32[128,512]{1,0:T(8,128)S(1)} %slice.40), channel_id=1, source_target_pairs={{16,0},{32,16},{48,32},{64,48},{80,64},{96,80},{112,96},{17,1},{33... | collective-permute-start | bytes 786440 | tf_op jit(solution)/shard_map/while/body/eval_jaxpr/ppermute | solution.py:12
  257.9 23.1 %collective-permute-start.1 = (f32[128,512]{1,0:T(8,128)S(1)}, f32[128,512]{1,0:T(8,128)S(1)}, u32[]{:S(2)}, u32[]{:S(2)}) collective-permute-start(f32[128,512]{1,0:T(8,128)S(1)} %get-tuple-element.288), channel_id=1, source_target_pairs={{0,16},{16,32},{32,48},{48,64},{64,80},{80,96},{96,112},{1,17},{17... | collective-permute-start | bytes 786440 | tf_op jit(solution)/shard_map/while/body/eval_jaxpr/ppermute | solution.py:12
  282.7 22.6 %collective-permute-start = (f32[128,512]{1,0:T(8,128)S(1)}, f32[128,512]{1,0:T(8,128)S(1)}, u32[]{:S(2)}, u32[]{:S(2)}) collective-permute-start(f32[128,512]{1,0:T(8,128)S(1)} %slice.40), channel_id=1, source_target_pairs={{16,0},{32,16},{48,32},{64,48},{80,64},{96,80},{112,96},{17,1},{33... | collective-permute-start | bytes 786440 | tf_op jit(solution)/shard_map/while/body/eval_jaxpr/ppermute | solution.py:12
  306.3 23.0 %collective-permute-start.1 = (f32[128,512]{1,0:T(8,128)S(1)}, f32[128,512]{1,0:T(8,128)S(1)}, u32[]{:S(2)}, u32[]{:S(2)}) collective-permute-start(f32[128,512]{1,0:T(8,128)S(1)} %get-tuple-element.288), channel_id=1, source_target_pairs={{0,16},{16,32},{32,48},{48,64},{64,80},{80,96},{96,112},{1,17},{17... | collective-permute-start | bytes 786440 | tf_op jit(solution)/shard_map/while/body/eval_jaxpr/ppermute | solution.py:12
  331.0 8.7 %collective-permute-start = (f32[128,512]{1,0:T(8,128)S(1)}, f32[128,512]{1,0:T(8,128)S(1)}, u32[]{:S(2)}, u32[]{:S(2)}) collective-permute-start(f32[128,512]{1,0:T(8,128)S(1)} %slice.40), channel_id=1, source_target_pairs={{16,0},{32,16},{48,32},{64,48},{80,64},{96,80},{112,96},{17,1},{33... | collective-permute-start | bytes 786440 | tf_op jit(solution)/shard_map/while/body/eval_jaxpr/ppermute | solution.py:12
  354.1 8.3 %collective-permute-start.1 = (f32[128,512]{1,0:T(8,128)S(1)}, f32[128,512]{1,0:T(8,128)S(1)}, u32[]{:S(2)}, u32[]{:S(2)}) collective-permute-start(f32[128,512]{1,0:T(8,128)S(1)} %get-tuple-element.288), channel_id=1, source_target_pairs={{0,16},{16,32},{32,48},{48,64},{64,80},{80,96},{96,112},{1,17},{17... | collective-permute-start | bytes 786440 | tf_op jit(solution)/shard_map/while/body/eval_jaxpr/ppermute | solution.py:12
  364.0 9.8 %collective-permute-start = (f32[128,512]{1,0:T(8,128)S(1)}, f32[128,512]{1,0:T(8,128)S(1)}, u32[]{:S(2)}, u32[]{:S(2)}) collective-permute-start(f32[128,512]{1,0:T(8,128)S(1)} %slice.40), channel_id=1, source_target_pairs={{16,0},{32,16},{48,32},{64,48},{80,64},{96,80},{112,96},{17,1},{33... | collective-permute-start | bytes 786440 | tf_op jit(solution)/shard_map/while/body/eval_jaxpr/ppermute | solution.py:12
  374.9 22.2 %collective-permute-start.1 = (f32[128,512]{1,0:T(8,128)S(1)}, f32[128,512]{1,0:T(8,128)S(1)}, u32[]{:S(2)}, u32[]{:S(2)}) collective-permute-start(f32[128,512]{1,0:T(8,128)S(1)} %get-tuple-element.288), channel_id=1, source_target_pairs={{0,16},{16,32},{32,48},{48,64},{64,80},{80,96},{96,112},{1,17},{17... | collective-permute-start | bytes 786440 | tf_op jit(solution)/shard_map/while/body/eval_jaxpr/ppermute | solution.py:12
  398.7 8.7 %collective-permute-start = (f32[128,512]{1,0:T(8,128)S(1)}, f32[128,512]{1,0:T(8,128)S(1)}, u32[]{:S(2)}, u32[]{:S(2)}) collective-permute-start(f32[128,512]{1,0:T(8,128)S(1)} %slice.40), channel_id=1, source_target_pairs={{16,0},{32,16},{48,32},{64,48},{80,64},{96,80},{112,96},{17,1},{33... | collective-permute-start | bytes 786440 | tf_op jit(solution)/shard_map/while/body/eval_jaxpr/ppermute | solution.py:12
  421.8 8.3 %collective-permute-start.1 = (f32[128,512]{1,0:T(8,128)S(1)}, f32[128,512]{1,0:T(8,128)S(1)}, u32[]{:S(2)}, u32[]{:S(2)}) collective-permute-start(f32[128,512]{1,0:T(8,128)S(1)} %get-tuple-element.288), channel_id=1, source_target_pairs={{0,16},{16,32},{32,48},{48,64},{64,80},{80,96},{96,112},{1,17},{17... | collective-permute-start | bytes 786440 | tf_op jit(solution)/shard_map/while/body/eval_jaxpr/ppermute | solution.py:12
  431.8 9.4 %collective-permute-start = (f32[128,512]{1,0:T(8,128)S(1)}, f32[128,512]{1,0:T(8,128)S(1)}, u32[]{:S(2)}, u32[]{:S(2)}) collective-permute-start(f32[128,512]{1,0:T(8,128)S(1)} %slice.40), channel_id=1, source_target_pairs={{16,0},{32,16},{48,32},{64,48},{80,64},{96,80},{112,96},{17,1},{33... | collective-permute-start | bytes 786440 | tf_op jit(solution)/shard_map/while/body/eval_jaxpr/ppermute | solution.py:12
  442.2 22.2 %collective-permute-start.1 = (f32[128,512]{1,0:T(8,128)S(1)}, f32[128,512]{1,0:T(8,128)S(1)}, u32[]{:S(2)}, u32[]{:S(2)}) collective-permute-start(f32[128,512]{1,0:T(8,128)S(1)} %get-tuple-element.288), channel_id=1, source_target_pairs={{0,16},{16,32},{32,48},{48,64},{64,80},{80,96},{96,112},{1,17},{17... | collective-permute-start | bytes 786440 | tf_op jit(solution)/shard_map/while/body/eval_jaxpr/ppermute | solution.py:12
  466.1 9.2 %collective-permute-start = (f32[128,512]{1,0:T(8,128)S(1)}, f32[128,512]{1,0:T(8,128)S(1)}, u32[]{:S(2)}, u32[]{:S(2)}) collective-permute-start(f32[128,512]{1,0:T(8,128)S(1)} %slice.40), channel_id=1, source_target_pairs={{16,0},{32,16},{48,32},{64,48},{80,64},{96,80},{112,96},{17,1},{33... | collective-permute-start | bytes 786440 | tf_op jit(solution)/shard_map/while/body/eval_jaxpr/ppermute | solution.py:12
  489.7 9.1 %collective-permute-start.1 = (f32[128,512]{1,0:T(8,128)S(1)}, f32[128,512]{1,0:T(8,128)S(1)}, u32[]{:S(2)}, u32[]{:S(2)}) collective-permute-start(f32[128,512]{1,0:T(8,128)S(1)} %get-tuple-element.288), channel_id=1, source_target_pairs={{0,16},{16,32},{32,48},{48,64},{64,80},{80,96},{96,112},{1,17},{17... | collective-permute-start | bytes 786440 | tf_op jit(solution)/shard_map/while/body/eval_jaxpr/ppermute | solution.py:12
  500.5 10.0 %collective-permute-start = (f32[128,512]{1,0:T(8,128)S(1)}, f32[128,512]{1,0:T(8,128)S(1)}, u32[]{:S(2)}, u32[]{:S(2)}) collective-permute-start(f32[128,512]{1,0:T(8,128)S(1)} %slice.40), channel_id=1, source_target_pairs={{16,0},{32,16},{48,32},{64,48},{80,64},{96,80},{112,96},{17,1},{33... | collective-permute-start | bytes 786440 | tf_op jit(solution)/shard_map/while/body/eval_jaxpr/ppermute | solution.py:12
  511.5 24.6 %collective-permute-start.1 = (f32[128,512]{1,0:T(8,128)S(1)}, f32[128,512]{1,0:T(8,128)S(1)}, u32[]{:S(2)}, u32[]{:S(2)}) collective-permute-start(f32[128,512]{1,0:T(8,128)S(1)} %get-tuple-element.288), channel_id=1, source_target_pairs={{0,16},{16,32},{32,48},{48,64},{64,80},{80,96},{96,112},{1,17},{17... | collective-permute-start | bytes 786440 | tf_op jit(solution)/shard_map/while/body/eval_jaxpr/ppermute | solution.py:12
  537.8 12.0 %collective-permute-start = (f32[128,512]{1,0:T(8,128)S(1)}, f32[128,512]{1,0:T(8,128)S(1)}, u32[]{:S(2)}, u32[]{:S(2)}) collective-permute-start(f32[128,512]{1,0:T(8,128)S(1)} %slice.40), channel_id=1, source_target_pairs={{16,0},{32,16},{48,32},{64,48},{80,64},{96,80},{112,96},{17,1},{33... | collective-permute-start | bytes 786440 | tf_op jit(solution)/shard_map/while/body/eval_jaxpr/ppermute | solution.py:12
  564.2 9.9 %collective-permute-start.1 = (f32[128,512]{1,0:T(8,128)S(1)}, f32[128,512]{1,0:T(8,128)S(1)}, u32[]{:S(2)}, u32[]{:S(2)}) collective-permute-start(f32[128,512]{1,0:T(8,128)S(1)} %get-tuple-element.288), channel_id=1, source_target_pairs={{0,16},{16,32},{32,48},{48,64},{64,80},{80,96},{96,112},{1,17},{17... | collective-permute-start | bytes 786440 | tf_op jit(solution)/shard_map/while/body/eval_jaxpr/ppermute | solution.py:12
  575.8 10.2 %collective-permute-start = (f32[128,512]{1,0:T(8,128)S(1)}, f32[128,512]{1,0:T(8,128)S(1)}, u32[]{:S(2)}, u32[]{:S(2)}) collective-permute-start(f32[128,512]{1,0:T(8,128)S(1)} %slice.40), channel_id=1, source_target_pairs={{16,0},{32,16},{48,32},{64,48},{80,64},{96,80},{112,96},{17,1},{33... | collective-permute-start | bytes 786440 | tf_op jit(solution)/shard_map/while/body/eval_jaxpr/ppermute | solution.py:12
  587.0 22.6 %collective-permute-start.1 = (f32[128,512]{1,0:T(8,128)S(1)}, f32[128,512]{1,0:T(8,128)S(1)}, u32[]{:S(2)}, u32[]{:S(2)}) collective-permute-start(f32[128,512]{1,0:T(8,128)S(1)} %get-tuple-element.288), channel_id=1, source_target_pairs={{0,16},{16,32},{32,48},{48,64},{64,80},{80,96},{96,112},{1,17},{17... | collective-permute-start | bytes 786440 | tf_op jit(solution)/shard_map/while/body/eval_jaxpr/ppermute | solution.py:12
  611.2 8.3 %collective-permute-start = (f32[128,512]{1,0:T(8,128)S(1)}, f32[128,512]{1,0:T(8,128)S(1)}, u32[]{:S(2)}, u32[]{:S(2)}) collective-permute-start(f32[128,512]{1,0:T(8,128)S(1)} %slice.40), channel_id=1, source_target_pairs={{16,0},{32,16},{48,32},{64,48},{80,64},{96,80},{112,96},{17,1},{33... | collective-permute-start | bytes 786440 | tf_op jit(solution)/shard_map/while/body/eval_jaxpr/ppermute | solution.py:12
  633.9 10.4 %collective-permute-start.1 = (f32[128,512]{1,0:T(8,128)S(1)}, f32[128,512]{1,0:T(8,128)S(1)}, u32[]{:S(2)}, u32[]{:S(2)}) collective-permute-start(f32[128,512]{1,0:T(8,128)S(1)} %get-tuple-element.288), channel_id=1, source_target_pairs={{0,16},{16,32},{32,48},{48,64},{64,80},{80,96},{96,112},{1,17},{17... | collective-permute-start | bytes 786440 | tf_op jit(solution)/shard_map/while/body/eval_jaxpr/ppermute | solution.py:12
  646.1 8.4 %collective-permute-start = (f32[128,512]{1,0:T(8,128)S(1)}, f32[128,512]{1,0:T(8,128)S(1)}, u32[]{:S(2)}, u32[]{:S(2)}) collective-permute-start(f32[128,512]{1,0:T(8,128)S(1)} %slice.40), channel_id=1, source_target_pairs={{16,0},{32,16},{48,32},{64,48},{80,64},{96,80},{112,96},{17,1},{33... | collective-permute-start | bytes 786440 | tf_op jit(solution)/shard_map/while/body/eval_jaxpr/ppermute | solution.py:12
  655.5 22.1 %collective-permute-start.1 = (f32[128,512]{1,0:T(8,128)S(1)}, f32[128,512]{1,0:T(8,128)S(1)}, u32[]{:S(2)}, u32[]{:S(2)}) collective-permute-start(f32[128,512]{1,0:T(8,128)S(1)} %get-tuple-element.288), channel_id=1, source_target_pairs={{0,16},{16,32},{32,48},{48,64},{64,80},{80,96},{96,112},{1,17},{17... | collective-permute-start | bytes 786440 | tf_op jit(solution)/shard_map/while/body/eval_jaxpr/ppermute | solution.py:12
  679.3 8.7 %collective-permute-start = (f32[128,512]{1,0:T(8,128)S(1)}, f32[128,512]{1,0:T(8,128)S(1)}, u32[]{:S(2)}, u32[]{:S(2)}) collective-permute-start(f32[128,512]{1,0:T(8,128)S(1)} %slice.40), channel_id=1, source_target_pairs={{16,0},{32,16},{48,32},{64,48},{80,64},{96,80},{112,96},{17,1},{33... | collective-permute-start | bytes 786440 | tf_op jit(solution)/shard_map/while/body/eval_jaxpr/ppermute | solution.py:12
  702.4 8.3 %collective-permute-start.1 = (f32[128,512]{1,0:T(8,128)S(1)}, f32[128,512]{1,0:T(8,128)S(1)}, u32[]{:S(2)}, u32[]{:S(2)}) collective-permute-start(f32[128,512]{1,0:T(8,128)S(1)} %get-tuple-element.288), channel_id=1, source_target_pairs={{0,16},{16,32},{32,48},{48,64},{64,80},{80,96},{96,112},{1,17},{17... | collective-permute-start | bytes 786440 | tf_op jit(solution)/shard_map/while/body/eval_jaxpr/ppermute | solution.py:12
Sparse Core Ops, SparseCore 0:
  11.4 66.0 all-gather.1
where the time goes:
time: 721 us; the launch traced here: 718 us
  waiting for transfers between devices  375 us (52%)
  starting transfers between devices  154 us (21%)
  matrix products  68.5 us (10%)
  local copies, waits for them, and re-layouts  64.8 us (9%)
  blocking collectives  23.7 us (3%)
  other arithmetic  16.9 us (2%)
  between operations  13.6 us (2%)
    ppermute x36, waiting for transfers between devices, shifted(): return lax.ppermute(block, axis, route)  333 us
    ppermute x36, starting transfers between devices, shifted(): return lax.ppermute(block, axis, route)  154 us
    all_gather x1, waiting for transfers between devices, per_device(): lax.all_gather(mirror_entries, 'col', axis=2, tiled=True)  42 us
    dot_general x6, matrix products, apply_block(): lax.dot_general(mirror_directions, mixed_terms, (((0,), (0,)), ((), ())),...  29.9 us
    all_gather x1, blocking collectives, per_device(): lax.all_gather(tau_coefficients, 'col', axis=2, tiled=True)  23.7 us
    dot_general x6, matrix products, apply_block(): jnp.dot(mirror_directions, window, precision=PRECISE, preferred_element_t...  23.3 us
    slice x18, local copies, waits for them, and re-layouts, advance(): below_rows = shifted(current[:width_rows], 'row', -1)  17.4 us
    cond x6, local copies, waits for them, and re-layouts  15.8 us
  transfers between devices with their start and end apart: 37, of which 37 were waited for; matrix products, arithmetic and copies ran while one was open for 0% of the time, Pallas kernels for 0%

commit v1 on v0

--- a/solution.py
+++ b/solution.py
@@ -4,6 +4,14 @@
 from jax.sharding import PartitionSpec as P
 
 PRECISE = lax.Precision.HIGHEST
+
+
+def fill_marks_up(xs, bus_axis):
+    aux = jax.lax.axis_size(bus_axis)
+    vec_out = jnp.stack(aux * [xs])
+    q_next = jax.lax.all_to_all(vec_out, bus_axis, 0, 0)
+    view_out = jnp.concatenate(q_next, axis=2)
+    return view_out
 
 
 def shifted(block, axis, distance):
@@ -56,7 +64,7 @@
 
 def per_device(eigen_basis_rows, mirror_entries, tau_coefficients, mirror_tallies):
     gathered, scale_all = (
-        lax.all_gather(mirror_entries, "col", axis=2, tiled=True),
+        fill_marks_up(mirror_entries, "col"),
         lax.all_gather(tau_coefficients, "col", axis=2, tiled=True),
     )
     householders = gathered[:, 0]

time: 721 us -> 760 us (1.054)
  blocking collectives: 23.7 us -> 107 us
  waiting for transfers between devices: 375 us -> 332 us
  between operations: 13.6 us -> 0.2 us
  starting transfers between devices: 154 us -> 162 us
    all_gather x1, blocking collectives: 23.7 us -> 107 us  [per_device(): lax.all_gather(tau_coefficients, 'col', axis=2, tiled=True)]
    all_gather x1 -> x0, waiting for transfers between devices: 42 us -> none  [per_device(): lax.all_gather(mirror_entries, 'col', axis=2, tiled=True)]
  transfers between devices with their start and end apart: 37 -> 37, of which waited for: 37 -> 36; matrix products, arithmetic and copies ran while one was open for 0% -> 0% of each run, Pallas kernels for 0% -> 0%
where the time goes in v1:
time: 760 us; the launch traced here: 757 us
  waiting for transfers between devices  332 us (44%)
  starting transfers between devices  162 us (21%)
  blocking collectives  107 us (14%)
  matrix products  68.5 us (9%)
  local copies, waits for them, and re-layouts  68.1 us (9%)
  other arithmetic  16.9 us (2%)
    ppermute x36, waiting for transfers between devices, shifted(): return lax.ppermute(block, axis, route)  332 us
    ppermute x36, starting transfers between devices, shifted(): return lax.ppermute(block, axis, route)  155 us
    all_gather x1, blocking collectives, per_device(): lax.all_gather(tau_coefficients, 'col', axis=2, tiled=True)  107 us
    dot_general x6, matrix products, apply_block(): lax.dot_general(mirror_directions, mixed_terms, (((0,), (0,)), ((), ())),...  29.9 us
    dot_general x6, matrix products, apply_block(): jnp.dot(mirror_directions, window, precision=PRECISE, preferred_element_t...  23.3 us
    slice x18, local copies, waits for them, and re-layouts, advance(): below_rows = shifted(current[:width_rows], 'row', -1)  17.4 us
    cond x6, local copies, waits for them, and re-layouts  15.8 us
  transfers between devices with their start and end apart: 37, of which 36 were waited for; matrix products, arithmetic and copies ran while one was open for 0% of the time, Pallas kernels for 0%

profile of v1, /device:TPU:98, one launch (start us, length us, event | category | flops | bytes accessed | tf_op | source)
XLA Modules:
  0.0 756.9 jit_solution(1854662041044715096)
XLA Ops:
  0.0 4.7 copy.30
  7.9 6.3 all-to-all-start
  14.4 107.5 %all_gather.3 = f32[6,1,128]{0,1,2:T(1,128)S(1)} all-gather(f32[6,1,8]{0,1,2:T(1,128)S(1)} %copy.11), channel_id=1, replica_groups=mesh['row'=8,'col'=16] {'col'}, dimensions={2}, use_global_device_ids=true | all-gather | bytes 3264 | tf_op jit(solution)/shard_map/all_gather | solution.py:68
  125.8 6.6 fusion.13
  138.9 617.9 %while.16 = (s32[]{:T(128)}, f32[2048,512]{1,0:T(8,128)}, s32[]{:T(128)}, f32[6,128,2176]{2,1,0:T(8,128)}, f32[6,128,128]{2,1,0:T(8,128)S(1)}, /*index=5*/s32[]{...) while((s32[]{:T(128)}, f32[2048,512]{1,0:T(8,128)}, s32[]{:T(128)}, ...), condition=%wide.region_3.4_spmd, body=%wide.region_0.3_spmd.sunk | while | flops 3524395008 | bytes 38470408 | solution.py:117
  139.9 8.8 %collective-permute-start = (f32[128,512]{1,0:T(8,128)S(1)}, f32[128,512]{1,0:T(8,128)S(1)}, u32[]{:S(2)}, u32[]{:S(2)}) collective-permute-start(f32[128,512]{1,0:T(8,128)S(1)} %slice.40), channel_id=1, source_target_pairs={{16,0},{32,16},{48,32},{64,48},{80,64},{96,80},{112,96},{17,1},{33... | collective-permute-start | bytes 786440 | tf_op jit(solution)/shard_map/while/body/eval_jaxpr/ppermute | solution.py:20
  148.8 6.0 collective-permute-done
  157.1 9.0 %collective-permute-done.1 = f32[128,512]{1,0:T(8,128)S(1)} collective-permute-done((f32[128,512]{1,0:T(8,128)S(1)}, f32[128,512]{1,0:T(8,128)S(1)}, u32[]{:S(2)}, u32[]{:S(2)}) %collective-permute-start.1) | collective-permute-done | bytes 262176 | tf_op jit(solution)/shard_map/while/body/eval_jaxpr/ppermute | solution.py:20
  167.9 4.6 collective-permute-start
  172.5 4.3 collective-permute-done
  179.1 7.4 collective-permute-done.1
  188.2 4.8 collective-permute-start
  199.2 7.4 collective-permute-done.1
  208.3 4.8 collective-permute-start
  219.4 11.7 %collective-permute-done.1 = f32[128,512]{1,0:T(8,128)S(1)} collective-permute-done((f32[128,512]{1,0:T(8,128)S(1)}, f32[128,512]{1,0:T(8,128)S(1)}, u32[]{:S(2)}, u32[]{:S(2)}) %collective-permute-start.1) | collective-permute-done | bytes 262176 | tf_op jit(solution)/shard_map/while/body/eval_jaxpr/ppermute | solution.py:20
  232.8 18.7 %collective-permute-start = (f32[128,512]{1,0:T(8,128)S(1)}, f32[128,512]{1,0:T(8,128)S(1)}, u32[]{:S(2)}, u32[]{:S(2)}) collective-permute-start(f32[128,512]{1,0:T(8,128)S(1)} %slice.40), channel_id=1, source_target_pairs={{16,0},{32,16},{48,32},{64,48},{80,64},{96,80},{112,96},{17,1},{33... | collective-permute-start | bytes 786440 | tf_op jit(solution)/shard_map/while/body/eval_jaxpr/ppermute | solution.py:20
  251.6 3.8 collective-permute-done
  257.7 22.9 %collective-permute-done.1 = f32[128,512]{1,0:T(8,128)S(1)} collective-permute-done((f32[128,512]{1,0:T(8,128)S(1)}, f32[128,512]{1,0:T(8,128)S(1)}, u32[]{:S(2)}, u32[]{:S(2)}) %collective-permute-start.1) | collective-permute-done | bytes 262176 | tf_op jit(solution)/shard_map/while/body/eval_jaxpr/ppermute | solution.py:20
  282.3 19.2 %collective-permute-start = (f32[128,512]{1,0:T(8,128)S(1)}, f32[128,512]{1,0:T(8,128)S(1)}, u32[]{:S(2)}, u32[]{:S(2)}) collective-permute-start(f32[128,512]{1,0:T(8,128)S(1)} %slice.40), channel_id=1, source_target_pairs={{16,0},{32,16},{48,32},{64,48},{80,64},{96,80},{112,96},{17,1},{33... | collective-permute-start | bytes 786440 | tf_op jit(solution)/shard_map/while/body/eval_jaxpr/ppermute | solution.py:20
  307.7 22.4 %collective-permute-done.1 = f32[128,512]{1,0:T(8,128)S(1)} collective-permute-done((f32[128,512]{1,0:T(8,128)S(1)}, f32[128,512]{1,0:T(8,128)S(1)}, u32[]{:S(2)}, u32[]{:S(2)}) %collective-permute-start.1) | collective-permute-done | bytes 262176 | tf_op jit(solution)/shard_map/while/body/eval_jaxpr/ppermute | solution.py:20
  331.8 18.7 %collective-permute-start = (f32[128,512]{1,0:T(8,128)S(1)}, f32[128,512]{1,0:T(8,128)S(1)}, u32[]{:S(2)}, u32[]{:S(2)}) collective-permute-start(f32[128,512]{1,0:T(8,128)S(1)} %slice.40), channel_id=1, source_target_pairs={{16,0},{32,16},{48,32},{64,48},{80,64},{96,80},{112,96},{17,1},{33... | collective-permute-start | bytes 786440 | tf_op jit(solution)/shard_map/while/body/eval_jaxpr/ppermute | solution.py:20
  356.7 20.8 %collective-permute-done.1 = f32[128,512]{1,0:T(8,128)S(1)} collective-permute-done((f32[128,512]{1,0:T(8,128)S(1)}, f32[128,512]{1,0:T(8,128)S(1)}, u32[]{:S(2)}, u32[]{:S(2)}) %collective-permute-start.1) | collective-permute-done | bytes 262176 | tf_op jit(solution)/shard_map/while/body/eval_jaxpr/ppermute | solution.py:20
  379.2 4.8 collective-permute-start
  387.9 14.4 %conditional.2 = (f32[2048,512]{1,0:T(8,128)}, f32[128,512]{1,0:T(8,128)S(1)}, f32[128,512]{1,0:T(8,128)S(1)}) conditional(s32[]{:T(128)} %convert_element_type.41, (f32[2048,512]{1,0:T(8,128)}, f32[128,512]{1,0:T(8,128)S(1)}) %tuple.59, (f32[2048,512]{1,0:T(8,128)}, f32[128,512]{1,0:T(8,128)S(1)}, s32[]{:T(128)}, f32[6,128,2176]{2,1,0:T(8,128)}, ...), branch_computations={%region_1.1_spmd, %region_2.2_spmd} | conditional | flops 3524329472 | bytes 35061820 | solution.py:110
  390.6 3.9 fusion.1
  394.8 5.0 convolution_subtract_fusion
  403.7 6.9 collective-permute-done.1
  412.3 4.8 collective-permute-start
  423.2 23.0 %collective-permute-done.1 = f32[128,512]{1,0:T(8,128)S(1)} collective-permute-done((f32[128,512]{1,0:T(8,128)S(1)}, f32[128,512]{1,0:T(8,128)S(1)}, u32[]{:S(2)}, u32[]{:S(2)}) %collective-permute-start.1) | collective-permute-done | bytes 262176 | tf_op jit(solution)/shard_map/while/body/eval_jaxpr/ppermute | solution.py:20
  448.0 4.8 collective-permute-start
  456.7 14.4 %conditional.2 = (f32[2048,512]{1,0:T(8,128)}, f32[128,512]{1,0:T(8,128)S(1)}, f32[128,512]{1,0:T(8,128)S(1)}) conditional(s32[]{:T(128)} %convert_element_type.41, (f32[2048,512]{1,0:T(8,128)}, f32[128,512]{1,0:T(8,128)S(1)}) %tuple.59, (f32[2048,512]{1,0:T(8,128)}, f32[128,512]{1,0:T(8,128)S(1)}, s32[]{:T(128)}, f32[6,128,2176]{2,1,0:T(8,128)}, ...), branch_computations={%region_1.1_spmd, %region_2.2_spmd} | conditional | flops 3524329472 | bytes 35061820 | solution.py:110
  459.3 3.9 fusion.1
  463.6 5.0 convolution_subtract_fusion
  472.4 6.9 collective-permute-done.1
  490.6 20.8 %collective-permute-done.1 = f32[128,512]{1,0:T(8,128)S(1)} collective-permute-done((f32[128,512]{1,0:T(8,128)S(1)}, f32[128,512]{1,0:T(8,128)S(1)}, u32[]{:S(2)}, u32[]{:S(2)}) %collective-permute-start.1) | collective-permute-done | bytes 262176 | tf_op jit(solution)/shard_map/while/body/eval_jaxpr/ppermute | solution.py:20
  513.1 4.8 collective-permute-start
  521.8 14.4 %conditional.2 = (f32[2048,512]{1,0:T(8,128)}, f32[128,512]{1,0:T(8,128)S(1)}, f32[128,512]{1,0:T(8,128)S(1)}) conditional(s32[]{:T(128)} %convert_element_type.41, (f32[2048,512]{1,0:T(8,128)}, f32[128,512]{1,0:T(8,128)S(1)}) %tuple.59, (f32[2048,512]{1,0:T(8,128)}, f32[128,512]{1,0:T(8,128)S(1)}, s32[]{:T(128)}, f32[6,128,2176]{2,1,0:T(8,128)}, ...), branch_computations={%region_1.1_spmd, %region_2.2_spmd} | conditional | flops 3524329472 | bytes 35061820 | solution.py:110
  524.5 3.9 fusion.1
  528.7 5.0 convolution_subtract_fusion
  537.5 6.9 collective-permute-done.1
  546.2 5.5 collective-permute-start
  557.9 20.8 %collective-permute-done.1 = f32[128,512]{1,0:T(8,128)S(1)} collective-permute-done((f32[128,512]{1,0:T(8,128)S(1)}, f32[128,512]{1,0:T(8,128)S(1)}, u32[]{:S(2)}, u32[]{:S(2)}) %collective-permute-start.1) | collective-permute-done | bytes 262176 | tf_op jit(solution)/shard_map/while/body/eval_jaxpr/ppermute | solution.py:20
  580.4 4.8 collective-permute-start
  585.3 4.1 collective-permute-done
  589.4 14.4 %conditional.2 = (f32[2048,512]{1,0:T(8,128)}, f32[128,512]{1,0:T(8,128)S(1)}, f32[128,512]{1,0:T(8,128)S(1)}) conditional(s32[]{:T(128)} %convert_element_type.41, (f32[2048,512]{1,0:T(8,128)}, f32[128,512]{1,0:T(8,128)S(1)}) %tuple.59, (f32[2048,512]{1,0:T(8,128)}, f32[128,512]{1,0:T(8,128)S(1)}, s32[]{:T(128)}, f32[6,128,2176]{2,1,0:T(8,128)}, ...), branch_computations={%region_1.1_spmd, %region_2.2_spmd} | conditional | flops 3524329472 | bytes 35061820 | solution.py:110
  592.1 3.9 fusion.1
  596.4 5.0 convolution_subtract_fusion
  605.2 7.6 collective-permute-done.1
  618.3 5.2 collective-permute-done
  625.8 23.8 %collective-permute-done.1 = f32[128,512]{1,0:T(8,128)S(1)} collective-permute-done((f32[128,512]{1,0:T(8,128)S(1)}, f32[128,512]{1,0:T(8,128)S(1)}, u32[]{:S(2)}, u32[]{:S(2)}) %collective-permute-start.1) | collective-permute-done | bytes 262176 | tf_op jit(solution)/shard_map/while/body/eval_jaxpr/ppermute | solution.py:20
  651.2 6.6 collective-permute-start
  657.9 5.7 collective-permute-done
  663.6 14.4 %conditional.2 = (f32[2048,512]{1,0:T(8,128)}, f32[128,512]{1,0:T(8,128)S(1)}, f32[128,512]{1,0:T(8,128)S(1)}) conditional(s32[]{:T(128)} %convert_element_type.41, (f32[2048,512]{1,0:T(8,128)}, f32[128,512]{1,0:T(8,128)S(1)}) %tuple.59, (f32[2048,512]{1,0:T(8,128)}, f32[128,512]{1,0:T(8,128)S(1)}, s32[]{:T(128)}, f32[6,128,2176]{2,1,0:T(8,128)}, ...), branch_computations={%region_1.1_spmd, %region_2.2_spmd} | conditional | flops 3524329472 | bytes 35061820 | solution.py:110
  666.3 3.9 fusion.1
  670.5 5.0 convolution_subtract_fusion
  679.3 8.7 %collective-permute-done.1 = f32[128,512]{1,0:T(8,128)S(1)} collective-permute-done((f32[128,512]{1,0:T(8,128)S(1)}, f32[128,512]{1,0:T(8,128)S(1)}, u32[]{:S(2)}, u32[]{:S(2)}) %collective-permute-start.1) | collective-permute-done | bytes 262176 | tf_op jit(solution)/shard_map/while/body/eval_jaxpr/ppermute | solution.py:20
  689.7 4.6 collective-permute-start
  694.3 5.6 collective-permute-done
  702.3 21.3 %collective-permute-done.1 = f32[128,512]{1,0:T(8,128)S(1)} collective-permute-done((f32[128,512]{1,0:T(8,128)S(1)}, f32[128,512]{1,0:T(8,128)S(1)}, u32[]{:S(2)}, u32[]{:S(2)}) %collective-permute-start.1) | collective-permute-done | bytes 262176 | tf_op jit(solution)/shard_map/while/body/eval_jaxpr/ppermute | solution.py:20
  725.3 4.4 collective-permute-start
  733.5 14.4 %conditional.2 = (f32[2048,512]{1,0:T(8,128)}, f32[128,512]{1,0:T(8,128)S(1)}, f32[128,512]{1,0:T(8,128)S(1)}) conditional(s32[]{:T(128)} %convert_element_type.41, (f32[2048,512]{1,0:T(8,128)}, f32[128,512]{1,0:T(8,128)S(1)}) %tuple.59, (f32[2048,512]{1,0:T(8,128)}, f32[128,512]{1,0:T(8,128)S(1)}, s32[]{:T(128)}, f32[6,128,2176]{2,1,0:T(8,128)}, ...), branch_computations={%region_1.1_spmd, %region_2.2_spmd} | conditional | flops 3524329472 | bytes 35061820 | solution.py:110
  736.1 3.9 fusion.1
  740.4 5.0 convolution_subtract_fusion
  749.2 6.9 collective-permute-done.1
  (154 shorter events, 173.0 us)
Async XLA Ops:
  0.0 4.7 copy-start.1
  7.9 6.3 copy-start.2
  7.9 6.4 copy-start.3
  7.9 114.3 %all-to-all-start = ((f32[16,6,1,8,2176]{4,3,1,2,0:T(8,128)}), f32[16,6,1,8,2176]{4,3,1,2,0:T(8,128)}, u32[]{:S(2)}, u32[]{:S(2)}) async-start(f32[16,6,1,8,2176]{4,3,1,2,0:T(8,128)} %stack.2), calls=%async_computation | async-start | bytes 13369344 | tf_op jit(solution)/shard_map/all_to_all | solution.py:12
  125.7 6.6 copy-start
  139.9 14.9 %collective-permute-start = (f32[128,512]{1,0:T(8,128)S(1)}, f32[128,512]{1,0:T(8,128)S(1)}, u32[]{:S(2)}, u32[]{:S(2)}) collective-permute-start(f32[128,512]{1,0:T(8,128)S(1)} %slice.40), channel_id=1, source_target_pairs={{16,0},{32,16},{48,32},{64,48},{80,64},{96,80},{112,96},{17,1},{33... | collective-permute-start | bytes 786440 | tf_op jit(solution)/shard_map/while/body/eval_jaxpr/ppermute | solution.py:20
  155.8 10.4 %collective-permute-start.1 = (f32[128,512]{1,0:T(8,128)S(1)}, f32[128,512]{1,0:T(8,128)S(1)}, u32[]{:S(2)}, u32[]{:S(2)}) collective-permute-start(f32[128,512]{1,0:T(8,128)S(1)} %get-tuple-element.288), channel_id=1, source_target_pairs={{0,16},{16,32},{32,48},{48,64},{64,80},{80,96},{96,112},{1,17},{17... | collective-permute-start | bytes 786440 | tf_op jit(solution)/shard_map/while/body/eval_jaxpr/ppermute | solution.py:20
  167.9 8.9 %collective-permute-start = (f32[128,512]{1,0:T(8,128)S(1)}, f32[128,512]{1,0:T(8,128)S(1)}, u32[]{:S(2)}, u32[]{:S(2)}) collective-permute-start(f32[128,512]{1,0:T(8,128)S(1)} %slice.40), channel_id=1, source_target_pairs={{16,0},{32,16},{48,32},{64,48},{80,64},{96,80},{112,96},{17,1},{33... | collective-permute-start | bytes 786440 | tf_op jit(solution)/shard_map/while/body/eval_jaxpr/ppermute | solution.py:20
  177.8 8.7 %collective-permute-start.1 = (f32[128,512]{1,0:T(8,128)S(1)}, f32[128,512]{1,0:T(8,128)S(1)}, u32[]{:S(2)}, u32[]{:S(2)}) collective-permute-start(f32[128,512]{1,0:T(8,128)S(1)} %get-tuple-element.288), channel_id=1, source_target_pairs={{0,16},{16,32},{32,48},{48,64},{64,80},{80,96},{96,112},{1,17},{17... | collective-permute-start | bytes 786440 | tf_op jit(solution)/shard_map/while/body/eval_jaxpr/ppermute | solution.py:20
  188.2 8.7 %collective-permute-start = (f32[128,512]{1,0:T(8,128)S(1)}, f32[128,512]{1,0:T(8,128)S(1)}, u32[]{:S(2)}, u32[]{:S(2)}) collective-permute-start(f32[128,512]{1,0:T(8,128)S(1)} %slice.40), channel_id=1, source_target_pairs={{16,0},{32,16},{48,32},{64,48},{80,64},{96,80},{112,96},{17,1},{33... | collective-permute-start | bytes 786440 | tf_op jit(solution)/shard_map/while/body/eval_jaxpr/ppermute | solution.py:20
  197.9 8.7 %collective-permute-start.1 = (f32[128,512]{1,0:T(8,128)S(1)}, f32[128,512]{1,0:T(8,128)S(1)}, u32[]{:S(2)}, u32[]{:S(2)}) collective-permute-start(f32[128,512]{1,0:T(8,128)S(1)} %get-tuple-element.288), channel_id=1, source_target_pairs={{0,16},{16,32},{32,48},{48,64},{64,80},{80,96},{96,112},{1,17},{17... | collective-permute-start | bytes 786440 | tf_op jit(solution)/shard_map/while/body/eval_jaxpr/ppermute | solution.py:20
  208.3 8.7 %collective-permute-start = (f32[128,512]{1,0:T(8,128)S(1)}, f32[128,512]{1,0:T(8,128)S(1)}, u32[]{:S(2)}, u32[]{:S(2)}) collective-permute-start(f32[128,512]{1,0:T(8,128)S(1)} %slice.40), channel_id=1, source_target_pairs={{16,0},{32,16},{48,32},{64,48},{80,64},{96,80},{112,96},{17,1},{33... | collective-permute-start | bytes 786440 | tf_op jit(solution)/shard_map/while/body/eval_jaxpr/ppermute | solution.py:20
  218.0 13.1 %collective-permute-start.1 = (f32[128,512]{1,0:T(8,128)S(1)}, f32[128,512]{1,0:T(8,128)S(1)}, u32[]{:S(2)}, u32[]{:S(2)}) collective-permute-start(f32[128,512]{1,0:T(8,128)S(1)} %get-tuple-element.288), channel_id=1, source_target_pairs={{0,16},{16,32},{32,48},{48,64},{64,80},{80,96},{96,112},{1,17},{17... | collective-permute-start | bytes 786440 | tf_op jit(solution)/shard_map/while/body/eval_jaxpr/ppermute | solution.py:20
  232.8 22.6 %collective-permute-start = (f32[128,512]{1,0:T(8,128)S(1)}, f32[128,512]{1,0:T(8,128)S(1)}, u32[]{:S(2)}, u32[]{:S(2)}) collective-permute-start(f32[128,512]{1,0:T(8,128)S(1)} %slice.40), channel_id=1, source_target_pairs={{16,0},{32,16},{48,32},{64,48},{80,64},{96,80},{112,96},{17,1},{33... | collective-permute-start | bytes 786440 | tf_op jit(solution)/shard_map/while/body/eval_jaxpr/ppermute | solution.py:20
  256.4 24.2 %collective-permute-start.1 = (f32[128,512]{1,0:T(8,128)S(1)}, f32[128,512]{1,0:T(8,128)S(1)}, u32[]{:S(2)}, u32[]{:S(2)}) collective-permute-start(f32[128,512]{1,0:T(8,128)S(1)} %get-tuple-element.288), channel_id=1, source_target_pairs={{0,16},{16,32},{32,48},{48,64},{64,80},{80,96},{96,112},{1,17},{17... | collective-permute-start | bytes 786440 | tf_op jit(solution)/shard_map/while/body/eval_jaxpr/ppermute | solution.py:20
  282.3 23.1 %collective-permute-start = (f32[128,512]{1,0:T(8,128)S(1)}, f32[128,512]{1,0:T(8,128)S(1)}, u32[]{:S(2)}, u32[]{:S(2)}) collective-permute-start(f32[128,512]{1,0:T(8,128)S(1)} %slice.40), channel_id=1, source_target_pairs={{16,0},{32,16},{48,32},{64,48},{80,64},{96,80},{112,96},{17,1},{33... | collective-permute-start | bytes 786440 | tf_op jit(solution)/shard_map/while/body/eval_jaxpr/ppermute | solution.py:20
  306.4 23.7 %collective-permute-start.1 = (f32[128,512]{1,0:T(8,128)S(1)}, f32[128,512]{1,0:T(8,128)S(1)}, u32[]{:S(2)}, u32[]{:S(2)}) collective-permute-start(f32[128,512]{1,0:T(8,128)S(1)} %get-tuple-element.288), channel_id=1, source_target_pairs={{0,16},{16,32},{32,48},{48,64},{64,80},{80,96},{96,112},{1,17},{17... | collective-permute-start | bytes 786440 | tf_op jit(solution)/shard_map/while/body/eval_jaxpr/ppermute | solution.py:20
  331.8 22.6 %collective-permute-start = (f32[128,512]{1,0:T(8,128)S(1)}, f32[128,512]{1,0:T(8,128)S(1)}, u32[]{:S(2)}, u32[]{:S(2)}) collective-permute-start(f32[128,512]{1,0:T(8,128)S(1)} %slice.40), channel_id=1, source_target_pairs={{16,0},{32,16},{48,32},{64,48},{80,64},{96,80},{112,96},{17,1},{33... | collective-permute-start | bytes 786440 | tf_op jit(solution)/shard_map/while/body/eval_jaxpr/ppermute | solution.py:20
  355.4 22.2 %collective-permute-start.1 = (f32[128,512]{1,0:T(8,128)S(1)}, f32[128,512]{1,0:T(8,128)S(1)}, u32[]{:S(2)}, u32[]{:S(2)}) collective-permute-start(f32[128,512]{1,0:T(8,128)S(1)} %get-tuple-element.288), channel_id=1, source_target_pairs={{0,16},{16,32},{32,48},{48,64},{64,80},{80,96},{96,112},{1,17},{17... | collective-permute-start | bytes 786440 | tf_op jit(solution)/shard_map/while/body/eval_jaxpr/ppermute | solution.py:20
  379.2 8.7 %collective-permute-start = (f32[128,512]{1,0:T(8,128)S(1)}, f32[128,512]{1,0:T(8,128)S(1)}, u32[]{:S(2)}, u32[]{:S(2)}) collective-permute-start(f32[128,512]{1,0:T(8,128)S(1)} %slice.40), channel_id=1, source_target_pairs={{16,0},{32,16},{48,32},{64,48},{80,64},{96,80},{112,96},{17,1},{33... | collective-permute-start | bytes 786440 | tf_op jit(solution)/shard_map/while/body/eval_jaxpr/ppermute | solution.py:20
  402.3 8.3 %collective-permute-start.1 = (f32[128,512]{1,0:T(8,128)S(1)}, f32[128,512]{1,0:T(8,128)S(1)}, u32[]{:S(2)}, u32[]{:S(2)}) collective-permute-start(f32[128,512]{1,0:T(8,128)S(1)} %get-tuple-element.288), channel_id=1, source_target_pairs={{0,16},{16,32},{32,48},{48,64},{64,80},{80,96},{96,112},{1,17},{17... | collective-permute-start | bytes 786440 | tf_op jit(solution)/shard_map/while/body/eval_jaxpr/ppermute | solution.py:20
  412.3 8.6 %collective-permute-start = (f32[128,512]{1,0:T(8,128)S(1)}, f32[128,512]{1,0:T(8,128)S(1)}, u32[]{:S(2)}, u32[]{:S(2)}) collective-permute-start(f32[128,512]{1,0:T(8,128)S(1)} %slice.40), channel_id=1, source_target_pairs={{16,0},{32,16},{48,32},{64,48},{80,64},{96,80},{112,96},{17,1},{33... | collective-permute-start | bytes 786440 | tf_op jit(solution)/shard_map/while/body/eval_jaxpr/ppermute | solution.py:20
  421.9 24.4 %collective-permute-start.1 = (f32[128,512]{1,0:T(8,128)S(1)}, f32[128,512]{1,0:T(8,128)S(1)}, u32[]{:S(2)}, u32[]{:S(2)}) collective-permute-start(f32[128,512]{1,0:T(8,128)S(1)} %get-tuple-element.288), channel_id=1, source_target_pairs={{0,16},{16,32},{32,48},{48,64},{64,80},{80,96},{96,112},{1,17},{17... | collective-permute-start | bytes 786440 | tf_op jit(solution)/shard_map/while/body/eval_jaxpr/ppermute | solution.py:20
  448.0 8.7 %collective-permute-start = (f32[128,512]{1,0:T(8,128)S(1)}, f32[128,512]{1,0:T(8,128)S(1)}, u32[]{:S(2)}, u32[]{:S(2)}) collective-permute-start(f32[128,512]{1,0:T(8,128)S(1)} %slice.40), channel_id=1, source_target_pairs={{16,0},{32,16},{48,32},{64,48},{80,64},{96,80},{112,96},{17,1},{33... | collective-permute-start | bytes 786440 | tf_op jit(solution)/shard_map/while/body/eval_jaxpr/ppermute | solution.py:20
  471.1 8.3 %collective-permute-start.1 = (f32[128,512]{1,0:T(8,128)S(1)}, f32[128,512]{1,0:T(8,128)S(1)}, u32[]{:S(2)}, u32[]{:S(2)}) collective-permute-start(f32[128,512]{1,0:T(8,128)S(1)} %get-tuple-element.288), channel_id=1, source_target_pairs={{0,16},{16,32},{32,48},{48,64},{64,80},{80,96},{96,112},{1,17},{17... | collective-permute-start | bytes 786440 | tf_op jit(solution)/shard_map/while/body/eval_jaxpr/ppermute | solution.py:20
  481.0 7.2 collective-permute-start
  489.2 22.2 %collective-permute-start.1 = (f32[128,512]{1,0:T(8,128)S(1)}, f32[128,512]{1,0:T(8,128)S(1)}, u32[]{:S(2)}, u32[]{:S(2)}) collective-permute-start(f32[128,512]{1,0:T(8,128)S(1)} %get-tuple-element.288), channel_id=1, source_target_pairs={{0,16},{16,32},{32,48},{48,64},{64,80},{80,96},{96,112},{1,17},{17... | collective-permute-start | bytes 786440 | tf_op jit(solution)/shard_map/while/body/eval_jaxpr/ppermute | solution.py:20
  513.1 8.7 %collective-permute-start = (f32[128,512]{1,0:T(8,128)S(1)}, f32[128,512]{1,0:T(8,128)S(1)}, u32[]{:S(2)}, u32[]{:S(2)}) collective-permute-start(f32[128,512]{1,0:T(8,128)S(1)} %slice.40), channel_id=1, source_target_pairs={{16,0},{32,16},{48,32},{64,48},{80,64},{96,80},{112,96},{17,1},{33... | collective-permute-start | bytes 786440 | tf_op jit(solution)/shard_map/while/body/eval_jaxpr/ppermute | solution.py:20
  536.2 8.3 %collective-permute-start.1 = (f32[128,512]{1,0:T(8,128)S(1)}, f32[128,512]{1,0:T(8,128)S(1)}, u32[]{:S(2)}, u32[]{:S(2)}) collective-permute-start(f32[128,512]{1,0:T(8,128)S(1)} %get-tuple-element.288), channel_id=1, source_target_pairs={{0,16},{16,32},{32,48},{48,64},{64,80},{80,96},{96,112},{1,17},{17... | collective-permute-start | bytes 786440 | tf_op jit(solution)/shard_map/while/body/eval_jaxpr/ppermute | solution.py:20
  546.2 9.4 %collective-permute-start = (f32[128,512]{1,0:T(8,128)S(1)}, f32[128,512]{1,0:T(8,128)S(1)}, u32[]{:S(2)}, u32[]{:S(2)}) collective-permute-start(f32[128,512]{1,0:T(8,128)S(1)} %slice.40), channel_id=1, source_target_pairs={{16,0},{32,16},{48,32},{64,48},{80,64},{96,80},{112,96},{17,1},{33... | collective-permute-start | bytes 786440 | tf_op jit(solution)/shard_map/while/body/eval_jaxpr/ppermute | solution.py:20
  556.6 22.2 %collective-permute-start.1 = (f32[128,512]{1,0:T(8,128)S(1)}, f32[128,512]{1,0:T(8,128)S(1)}, u32[]{:S(2)}, u32[]{:S(2)}) collective-permute-start(f32[128,512]{1,0:T(8,128)S(1)} %get-tuple-element.288), channel_id=1, source_target_pairs={{0,16},{16,32},{32,48},{48,64},{64,80},{80,96},{96,112},{1,17},{17... | collective-permute-start | bytes 786440 | tf_op jit(solution)/shard_map/while/body/eval_jaxpr/ppermute | solution.py:20
  580.4 9.0 %collective-permute-start = (f32[128,512]{1,0:T(8,128)S(1)}, f32[128,512]{1,0:T(8,128)S(1)}, u32[]{:S(2)}, u32[]{:S(2)}) collective-permute-start(f32[128,512]{1,0:T(8,128)S(1)} %slice.40), channel_id=1, source_target_pairs={{16,0},{32,16},{48,32},{64,48},{80,64},{96,80},{112,96},{17,1},{33... | collective-permute-start | bytes 786440 | tf_op jit(solution)/shard_map/while/body/eval_jaxpr/ppermute | solution.py:20
  603.8 8.9 %collective-permute-start.1 = (f32[128,512]{1,0:T(8,128)S(1)}, f32[128,512]{1,0:T(8,128)S(1)}, u32[]{:S(2)}, u32[]{:S(2)}) collective-permute-start(f32[128,512]{1,0:T(8,128)S(1)} %get-tuple-element.288), channel_id=1, source_target_pairs={{0,16},{16,32},{32,48},{48,64},{64,80},{80,96},{96,112},{1,17},{17... | collective-permute-start | bytes 786440 | tf_op jit(solution)/shard_map/while/body/eval_jaxpr/ppermute | solution.py:20
  614.4 9.0 %collective-permute-start = (f32[128,512]{1,0:T(8,128)S(1)}, f32[128,512]{1,0:T(8,128)S(1)}, u32[]{:S(2)}, u32[]{:S(2)}) collective-permute-start(f32[128,512]{1,0:T(8,128)S(1)} %slice.40), channel_id=1, source_target_pairs={{16,0},{32,16},{48,32},{64,48},{80,64},{96,80},{112,96},{17,1},{33... | collective-permute-start | bytes 786440 | tf_op jit(solution)/shard_map/while/body/eval_jaxpr/ppermute | solution.py:20
  624.4 25.1 %collective-permute-start.1 = (f32[128,512]{1,0:T(8,128)S(1)}, f32[128,512]{1,0:T(8,128)S(1)}, u32[]{:S(2)}, u32[]{:S(2)}) collective-permute-start(f32[128,512]{1,0:T(8,128)S(1)} %get-tuple-element.288), channel_id=1, source_target_pairs={{0,16},{16,32},{32,48},{48,64},{64,80},{80,96},{96,112},{1,17},{17... | collective-permute-start | bytes 786440 | tf_op jit(solution)/shard_map/while/body/eval_jaxpr/ppermute | solution.py:20
  651.2 12.3 %collective-permute-start = (f32[128,512]{1,0:T(8,128)S(1)}, f32[128,512]{1,0:T(8,128)S(1)}, u32[]{:S(2)}, u32[]{:S(2)}) collective-permute-start(f32[128,512]{1,0:T(8,128)S(1)} %slice.40), channel_id=1, source_target_pairs={{16,0},{32,16},{48,32},{64,48},{80,64},{96,80},{112,96},{17,1},{33... | collective-permute-start | bytes 786440 | tf_op jit(solution)/shard_map/while/body/eval_jaxpr/ppermute | solution.py:20
  678.0 10.0 %collective-permute-start.1 = (f32[128,512]{1,0:T(8,128)S(1)}, f32[128,512]{1,0:T(8,128)S(1)}, u32[]{:S(2)}, u32[]{:S(2)}) collective-permute-start(f32[128,512]{1,0:T(8,128)S(1)} %get-tuple-element.288), channel_id=1, source_target_pairs={{0,16},{16,32},{32,48},{48,64},{64,80},{80,96},{96,112},{1,17},{17... | collective-permute-start | bytes 786440 | tf_op jit(solution)/shard_map/while/body/eval_jaxpr/ppermute | solution.py:20
  689.7 10.2 %collective-permute-start = (f32[128,512]{1,0:T(8,128)S(1)}, f32[128,512]{1,0:T(8,128)S(1)}, u32[]{:S(2)}, u32[]{:S(2)}) collective-permute-start(f32[128,512]{1,0:T(8,128)S(1)} %slice.40), channel_id=1, source_target_pairs={{16,0},{32,16},{48,32},{64,48},{80,64},{96,80},{112,96},{17,1},{33... | collective-permute-start | bytes 786440 | tf_op jit(solution)/shard_map/while/body/eval_jaxpr/ppermute | solution.py:20
  700.9 22.6 %collective-permute-start.1 = (f32[128,512]{1,0:T(8,128)S(1)}, f32[128,512]{1,0:T(8,128)S(1)}, u32[]{:S(2)}, u32[]{:S(2)}) collective-permute-start(f32[128,512]{1,0:T(8,128)S(1)} %get-tuple-element.288), channel_id=1, source_target_pairs={{0,16},{16,32},{32,48},{48,64},{64,80},{80,96},{96,112},{1,17},{17... | collective-permute-start | bytes 786440 | tf_op jit(solution)/shard_map/while/body/eval_jaxpr/ppermute | solution.py:20
  725.3 8.2 %collective-permute-start = (f32[128,512]{1,0:T(8,128)S(1)}, f32[128,512]{1,0:T(8,128)S(1)}, u32[]{:S(2)}, u32[]{:S(2)}) collective-permute-start(f32[128,512]{1,0:T(8,128)S(1)} %slice.40), channel_id=1, source_target_pairs={{16,0},{32,16},{48,32},{64,48},{80,64},{96,80},{112,96},{17,1},{33... | collective-permute-start | bytes 786440 | tf_op jit(solution)/shard_map/while/body/eval_jaxpr/ppermute | solution.py:20
  747.9 8.3 %collective-permute-start.1 = (f32[128,512]{1,0:T(8,128)S(1)}, f32[128,512]{1,0:T(8,128)S(1)}, u32[]{:S(2)}, u32[]{:S(2)}) collective-permute-start(f32[128,512]{1,0:T(8,128)S(1)} %get-tuple-element.288), channel_id=1, source_target_pairs={{0,16},{16,32},{32,48},{48,64},{64,80},{80,96},{96,112},{1,17},{17... | collective-permute-start | bytes 786440 | tf_op jit(solution)/shard_map/while/body/eval_jaxpr/ppermute | solution.py:20
